TPU v7x, 32 devices: a whole 2x2x4 slice. The times are simulated.
32 devices in a mesh: obs: 4 (over y, x), space: 8 (over z, core).
Axes of the slice: x: 2, y: 2, z: 4, core: 2. Of those that a mesh axis runs over, the one named last changes fastest.
Arguments:
- probes: float32 [32, 4, 128, 256], P(None, None, 'space'), may hold values from -6 to 6
- wind: float32 [4, 2, 2, 4, 128, 256], P('obs', None, None, None, 'space'), may hold values from -0.6 to 0.6
- station_cell: int32 [4, 2048], P('obs', 'space'), may hold values from 0 to 16383
- obs_count: int32 [4, 8], P('obs', 'space'), may hold values from 1 to 256, as said below
- obs_weight: float32 [4, 2048], P('obs', 'space'), may hold values from 0.5 to 4
Outputs:
- basis: float32 [32, 4, 128, 256], P('obs', None, 'space')
- core: float32 [32, 32], replicated
Inputs may be any that keep to these rules, and one draw needn't show every extreme that they name: `obs_count`: the live slots of a tile in a window are its first ones; some tile of some window has all 256 live.
All inputs are finite; a program needn't handle non-finite values.
Results may differ from a plain program's by a relative error of at most 0.0003.
Values sent between devices are 32-bit elements; how exact they have to be, the bound alone decides.
A program may use at most 64 MiB of HBM per device.

v0:
```python
import math

import jax
import jax.numpy as jnp
from jax import lax
from jax.sharding import PartitionSpec as P


def extended_2(block, sides, width):
    for axis, dim in sides:
        count = lax.axis_size(axis)
        forward = [(i, i + 1) for i in range(count - 1)]
        backward = [(target, source) for source, target in forward]
        low = lax.ppermute(
            lax.slice_in_dim(block, block.shape[dim] - width, None, axis=dim), axis, forward
        )
        high = lax.ppermute(lax.slice_in_dim(block, 0, width, axis=dim), axis, backward)
        block = jnp.concatenate([low, block, high], axis=dim)
    return block


def smooth_terms(centre, upper, lower):
    yplus = jnp.pad(centre, [(0, 0), (0, 0), (0, 0), (0, 1)])[:, :, :, 1:]
    yminus = jnp.pad(centre, [(0, 0), (0, 0), (0, 0), (1, 0)])[:, :, :, :-1]
    zplus = jnp.pad(centre, [(0, 0), (0, 1), (0, 0), (0, 0)])[:, 1:]
    zminus = jnp.pad(centre, [(0, 0), (1, 0), (0, 0), (0, 0)])[:, :-1]
    return (
        centre
        + 0.15 * (upper + lower + yplus + yminus - 4.0 * centre)
        + 0.1 * (zplus + zminus - 2.0 * centre),
        yplus,
        yminus,
    )


def forward_advance(extended, wind_x, wind_y):
    centre = extended[:, :, 1:-1]
    upper = extended[:, :, 2:]
    lower = extended[:, :, :-2]
    result, yplus, yminus = smooth_terms(centre, upper, lower)
    return result - 0.5 * (wind_x * (upper - lower) + wind_y * (yplus - yminus))


def adjoint_advance(extended, wind_x_ext, wind_y):
    centre = extended[:, :, 1:-1]
    upper = extended[:, :, 2:]
    lower = extended[:, :, :-2]
    result, yplus, yminus = smooth_terms(centre, upper, lower)
    carried = wind_x_ext * extended
    across = wind_y * centre
    aplus = jnp.pad(across, [(0, 0), (0, 0), (0, 0), (0, 1)])[:, :, :, 1:]
    aminus = jnp.pad(across, [(0, 0), (0, 0), (0, 0), (1, 0)])[:, :, :, :-1]
    return result + 0.5 * (carried[:, :, 2:] - carried[:, :, :-2] + (aplus - aminus))


def on_device(probes, wind, station_cell, obs_count, obs_weight):
    probe_count, levels, local_rows, columns = probes.shape
    steps = wind.shape[1]
    total_rows = local_rows * lax.axis_size("space")
    winds = wind[0]
    depth = 1
    wind_ext = extended_2(winds, (("space", 3),), depth)
    field = probes
    for step in range(steps):
        extended = extended_2(field, (("space", 2),), 1)
        field = forward_advance(
            extended,
            wind_ext[step, 0, :, 1 : 1 + local_rows],
            wind_ext[step, 1, :, 1 : 1 + local_rows],
        )
    slots = station_cell.shape[1]
    cells = station_cell[0]
    live = (lax.iota(jnp.int32, slots) < obs_count[0, 0]).astype(jnp.float32)
    flat = field.reshape(probe_count, -1)
    sampled = flat[:, cells]
    weighted = sampled * (obs_weight[0] * live)[None, :]
    injected = jnp.zeros_like(flat).at[:, cells].add(weighted).reshape(probes.shape)
    adjoint_field = injected
    for step in reversed(range(steps)):
        extended = extended_2(adjoint_field, (("space", 2),), 1)
        adjoint_field = adjoint_advance(
            extended,
            wind_ext[step, 0, :, 0 : local_rows + 2],
            wind_ext[step, 1, :, 1 : 1 + local_rows],
        )
    local_sketch = adjoint_field.reshape(probe_count, -1)
    omega = probes.reshape(probe_count, -1)
    divisor = lax.axis_size("obs") * lax.axis_size("space") * slots
    scale = math.sqrt(levels * total_rows * columns)
    rows_each = probe_count // lax.axis_size("obs")
    share = lax.psum_scatter(local_sketch, "obs", scatter_dimension=1, tiled=True)
    share_width = share.shape[1]
    omega_share = lax.dynamic_slice_in_dim(
        omega, lax.axis_index("obs") * share_width, share_width, 1
    )
    gram_part = jnp.dot(share, share.T, precision=lax.Precision.HIGHEST)
    cross_part = jnp.dot(omega_share, share.T, precision=lax.Precision.HIGHEST)
    gram, cross = lax.psum((gram_part, cross_part), ("obs", "space"))
    lower = jnp.linalg.cholesky(gram)
    basis_share = jax.scipy.linalg.solve_triangular(lower, share, lower=True) * scale
    basis = lax.all_to_all(basis_share, "obs", split_axis=0, concat_axis=1, tiled=True)
    core = cross / divisor
    return (basis.reshape(rows_each, levels, local_rows, columns), core)


def solution(mesh):
    in_specs = (
        P(None, None, "space", None),
        P("obs", None, None, None, "space", None),
        P("obs", "space"),
        P("obs", "space"),
        P("obs", "space"),
    )
    out_specs = (P("obs", None, "space", None), P())
    return jax.shard_map(
        on_device, mesh=mesh, in_specs=in_specs, out_specs=out_specs, check_vma=False
    )
```

profile of v0, /device:TPU:0, one launch (start us, length us, event | category | flops | bytes accessed | tf_op | source)
XLA Modules:
  0.0 184.4 jit_solution(10899908487729040925)
XLA Ops:
  7.2 2.8 %copy.76 = f32[32,4,16,256]{3,0,2,1:T(8,128)S(1)} copy(f32[32,4,16,256]{3,2,1,0:T(8,128)} %param.5) | data formatting | bytes 4194304 | tf_op args[0]
  11.4 3.0 %collective-permute-start.1 = (f32[32,4,1,256]{3,0,2,1:T(8,128)S(1)}, f32[32,4,1,256]{3,0,2,1:T(8,128)S(1)}, u32[]{:S(2)}, u32[]{:S(2)}) collective-permute-start(f32[32,4,1,256]{3,0,2,1:T(8,128)S(1)} %get-tuple-element.12), channel_id=1, source_target_pairs={{0,1},{1,2},{2,3},{3,4},{4,5},{5,6},{6,7},{8,9},{9,10},{10,11},{11... | collective-permute-start | bytes 393224 | tf_op jit(solution)/shard_map/ppermute | solution.py:14
  14.5 4.5 %collective-permute-start.6 = (f32[2,2,4,1,256]{4,3,2,1,0:T(1,128)S(1)}, f32[2,2,4,1,256]{4,3,2,1,0:T(1,128)S(1)}, u32[]{:S(2)}, u32[]{:S(2)}) collective-permute-start(f32[2,2,4,1,256]{4,3,2,1,0:T(1,128)S(1)} %get-tuple-element.16), channel_id=1, source_target_pairs={{0,1},{1,2},{2,3},{3,4},{4,5},{5,6},{6,7},{8,9},{9,10},{10,11},{11... | collective-permute-start | bytes 49160 | tf_op jit(solution)/shard_map/ppermute | solution.py:14
  21.1 2.5 %fusion.7 = f32[32,4,16,256]{3,0,2,1:T(8,128)S(1)} fusion(f32[32,4,16,256]{3,0,2,1:T(8,128)S(1)} %copy.76, f32[32,4,1,256]{3,0,2,1:T(8,128)S(1)} %collective-permute-done, f32[32,4,1,256]{3,0,2,1:T(8,128)S(1)} %collective-permute-done.1, f32[4,16,256]{2,1,0:T(8,128)S(1)} %get-tuple-element.20, f32[4,16,256]{2,1,0:T(8,128)S(1)} %get-tuple-element.21), kind=kLoop, calls=%fused_computation.32 | loop fusion | flops 11010048 | bytes 4587520 | tf_op jit(solution)/shard_map/sub | solution.py:41
  24.9 3.7 %collective-permute-start.3 = (f32[32,4,1,256]{3,0,2,1:T(8,128)S(1)}, f32[32,4,1,256]{3,0,2,1:T(8,128)S(1)}, u32[]{:S(2)}, u32[]{:S(2)}) collective-permute-start(f32[32,4,1,256]{3,0,2,1:T(8,128)S(1)} %get-tuple-element.10), channel_id=1, source_target_pairs={{0,1},{1,2},{2,3},{3,4},{4,5},{5,6},{6,7},{8,9},{9,10},{10,11},{11... | collective-permute-start | bytes 393224 | tf_op jit(solution)/shard_map/ppermute | solution.py:14
  29.6 2.5 %fusion.12 = f32[32,4,16,256]{3,0,2,1:T(8,128)S(1)} fusion(f32[32,4,16,256]{3,0,2,1:T(8,128)S(1)} %fusion.7, f32[32,4,1,256]{3,0,2,1:T(8,128)S(1)} %collective-permute-done.2, f32[32,4,1,256]{3,0,2,1:T(8,128)S(1)} %collective-permute-done.3, f32[4,16,256]{2,1,0:T(8,128)S(1)} %get-tuple-element.19, f32[4,16,256]{2,1,0:T(8,128)S(1)} %get-tuple-element.18), kind=kLoop, calls=%fused_computation.37 | loop fusion | flops 11010048 | bytes 4587520 | tf_op jit(solution)/shard_map/sub | solution.py:41
  32.0 4.7 %copy.80 = f32[32,4,16,256]{0,3,2,1:T(8,128)} copy(f32[32,4,16,256]{3,0,2,1:T(8,128)S(1)} %fusion.12) | data formatting | bytes 4194304 | tf_op jit(solution)/shard_map/sub | solution.py:41
  36.7 7.0 %scatter_custom_fusion = f32[32,16384]{0,1:T(8,128)} fusion(s32[256]{0:T(256)S(1)} %bitcast.65, f32[]{:T(128)} %constant.59.clone.1, f32[256]{0:T(256)S(1)} %bitcast.63, f32[32,16384]{0,1:T(8,128)} %bitcast.52, s32[1024]{0:T(1024)S(1)} %pad_clamp_fusion), kind=kCustom, calls=%fused_computation.4 | custom fusion | flops 16384 | bytes 4199428 | tf_op jit(solution)/shard_map/scatter-add | solution.py:77
  43.7 5.1 %copy.88 = f32[32,4,16,256]{3,0,2,1:T(8,128)S(1)} copy(f32[32,4,16,256]{0,3,2,1:T(8,128)} %bitcast.53) | data formatting | bytes 4194304 | tf_op jit(solution)/shard_map/reshape | solution.py:77
  50.1 5.2 %collective-permute-start.5 = (f32[32,4,1,256]{3,0,2,1:T(8,128)S(1)}, f32[32,4,1,256]{3,0,2,1:T(8,128)S(1)}, u32[]{:S(2)}, u32[]{:S(2)}) collective-permute-start(f32[32,4,1,256]{3,0,2,1:T(8,128)S(1)} %get-tuple-element.8), channel_id=1, source_target_pairs={{0,1},{1,2},{2,3},{3,4},{4,5},{5,6},{6,7},{8,9},{9,10},{10,11},{11... | collective-permute-start | bytes 393224 | tf_op jit(solution)/shard_map/ppermute | solution.py:14
  56.7 3.0 %broadcast_multiply_fusion.1 = (f32[32,4,16,256]{3,0,2,1:T(8,128)S(1)}, f32[32,4,16,256]{3,0,2,1:T(8,128)S(1)}) fusion(f32[4,16,256]{2,1,0:T(8,128)S(1)} %get-tuple-element.20, f32[32,4,16,256]{3,0,2,1:T(8,128)S(1)} %broadcast_multiply_fusion, f32[32,4,18,256]{3,0,2,1:T(8,128)S(1)} %maximum_multiply_fusion, f32[32,4,16,256]{3,0,2,1:T(8,128)S(1)} %copy.88, ...), kind=kLoop, calls=%fused_computation.77 | loop fusion | flops 10485760 | bytes 12910592 | tf_op jit(solution)/shard_map/mul | solution.py:50
  61.0 6.1 %collective-permute-start.9 = (f32[32,4,1,256]{3,0,2,1:T(8,128)S(1)}, f32[32,4,1,256]{3,0,2,1:T(8,128)S(1)}, u32[]{:S(2)}, u32[]{:S(2)}) collective-permute-start(f32[32,4,1,256]{3,0,2,1:T(8,128)S(1)} %get-tuple-element.6), channel_id=1, source_target_pairs={{0,1},{1,2},{2,3},{3,4},{4,5},{5,6},{6,7},{8,9},{9,10},{10,11},{11... | collective-permute-start | bytes 393224 | tf_op jit(solution)/shard_map/ppermute | solution.py:14
  68.3 3.0 %fusion.22 = f32[32,4,16,256]{3,0,2,1:T(8,128)S(1)} fusion(f32[32,4,16,256]{3,0,2,1:T(8,128)S(1)} %get-tuple-element.5, f32[32,4,16,256]{3,0,2,1:T(8,128)S(1)} %get-tuple-element.4, f32[32,4,18,256]{3,0,2,1:T(8,128)S(1)} %maximum_multiply_fusion.1, f32[32,4,1,256]{3,0,2,1:T(8,128)S(1)} %collective-permute-done.9, f32[32,4,1,256]{3,0,2,1:T(8,128)S(1)} %collective-permute-done.8), kind=kLoop, calls=%fused_computation.47 | loop fusion | flops 9961472 | bytes 10747904 | tf_op jit(solution)/shard_map/add | solution.py:53
  71.3 1.5 copy.100
  72.8 1.6 copy-done
  74.4 2.5 %copy.102 = f32[4,8,64,256]{3,1,2,0:T(8,128)} copy(f32[4,8,64,256]{3,2,1,0:T(8,128)S(1)} %bitcast.54) | data formatting | bytes 4194304
  76.9 36.7 %reduce-scatter.2.cloned.1.call-done = f32[32,4096]{1,0:T(8,128)} async-done(((f32[32,16384]{1,0:T(8,128)}), f32[32,4096]{1,0:T(8,128)}) %reduce-scatter.2.cloned.1.call-update) | async-done | bytes 524304 | tf_op jit(solution)/shard_map/reduce_scatter | solution.py:91
  113.6 1.8 fusion.57
  115.4 1.8 fusion.41
  117.2 39.6 %all-reduce.20 = (f32[32,32]{0,1:T(8,128)S(1)}, f32[32,32]{1,0:T(8,128)S(1)}) all-reduce(f32[32,32]{0,1:T(8,128)S(1)} %fusion.57, f32[32,32]{1,0:T(8,128)S(1)} %fusion.41), channel_id=1, replica_groups=mesh['obs'=4,'space'=8] {'obs','space'}, use_global_device_ids=true, to_apply=%region_2.3 | all-reduce | flops 2048 | bytes 16384 | tf_op jit(solution)/shard_map/psum | solution.py:98
  156.9 2.9 %cholesky.16 = f32[32,32]{1,0:T(8,128)S(1)} custom-call(f32[32,32]{1,0:T(8,128)S(1)} %fusion.48), custom_call_target="Cholesky" | custom-call | tf_op jit(solution)/shard_map/jit(cholesky)/cholesky | solution.py:99
  161.1 2.4 %custom-call.7 = f32[1,32,32]{1,2,0:T(8,128)S(1)} custom-call(f32[1,32,32]{2,1,0:T(8,128)S(1)} %fusion.46), custom_call_target="InvertDiagBlocksLowerTriangular" | custom-call | tf_op jit(solution)/shard_map/jit(_solve_triangular)/triangular_solve | solution.py:100
  165.0 4.4 %all-to-all-start = ((f32[4,8,4096]{2,1,0:T(8,128)}), f32[4,8,4096]{2,1,0:T(8,128)S(1)}, u32[]{:S(2)}, u32[]{:S(2)}) async-start(f32[4,8,4096]{2,1,0:T(8,128)} %fusion), calls=%async_computation.1 | async-start | bytes 1048576 | tf_op jit(solution)/shard_map/all_to_all | solution.py:101
  170.1 6.5 %all-to-all-done = f32[4,8,4096]{2,1,0:T(8,128)S(1)} async-done(((f32[4,8,4096]{2,1,0:T(8,128)}), f32[4,8,4096]{2,1,0:T(8,128)S(1)}, u32[]{:S(2)}, u32[]{:S(2)}) %all-to-all-start) | async-done | bytes 524320 | tf_op jit(solution)/shard_map/all_to_all | solution.py:101
  (48 shorter events, 14.4 us)
Async XLA Ops:
  7.2 7.3 %copy-start.2 = (f32[1,2,2,4,16,256]{5,4,3,2,1,0:T(8,128)S(1)}, f32[1,2,2,4,16,256]{5,4,3,2,1,0:T(8,128)}, u32[]{:S(2)}) copy-start(f32[1,2,2,4,16,256]{5,4,3,2,1,0:T(8,128)} %param.6) | copy-start | bytes 786436
  7.2 13.2 %copy-start.3 = (s32[1,256]{1,0:T(1,128)S(1)}, s32[1,256]{1,0:T(1,128)}, u32[]{:S(2)}) copy-start(s32[1,256]{1,0:T(1,128)} %param.7) | copy-start | bytes 3076
  7.2 13.9 %copy-start.4 = (f32[1,256]{1,0:T(1,128)S(1)}, f32[1,256]{1,0:T(1,128)}, u32[]{:S(2)}) copy-start(f32[1,256]{1,0:T(1,128)} %param.9) | copy-start | bytes 3076
  7.2 106.4 %reduce-scatter.2.cloned.1.call-start = ((), (), s32[]{:S(2)}) async-start(), calls=%async_computation.2 | async-start | bytes 2621440 | tf_op jit(solution)/shard_map/reduce_scatter | solution.py:91
  10.1 11.0 %collective-permute-start = (f32[32,4,1,256]{3,0,2,1:T(8,128)S(1)}, f32[32,4,1,256]{3,0,2,1:T(8,128)S(1)}, u32[]{:S(2)}, u32[]{:S(2)}) collective-permute-start(f32[32,4,1,256]{3,0,2,1:T(8,128)S(1)} %get-tuple-element.13), channel_id=1, source_target_pairs={{1,0},{2,1},{3,2},{4,3},{5,4},{6,5},{7,6},{9,8},{10,9},{11,10},{12... | collective-permute-start | bytes 393224 | tf_op jit(solution)/shard_map/ppermute | solution.py:17
  11.4 9.7 %collective-permute-start.1 = (f32[32,4,1,256]{3,0,2,1:T(8,128)S(1)}, f32[32,4,1,256]{3,0,2,1:T(8,128)S(1)}, u32[]{:S(2)}, u32[]{:S(2)}) collective-permute-start(f32[32,4,1,256]{3,0,2,1:T(8,128)S(1)} %get-tuple-element.12), channel_id=1, source_target_pairs={{0,1},{1,2},{2,3},{3,4},{4,5},{5,6},{6,7},{8,9},{9,10},{10,11},{11... | collective-permute-start | bytes 393224 | tf_op jit(solution)/shard_map/ppermute | solution.py:14
  14.5 14.1 %collective-permute-start.6 = (f32[2,2,4,1,256]{4,3,2,1,0:T(1,128)S(1)}, f32[2,2,4,1,256]{4,3,2,1,0:T(1,128)S(1)}, u32[]{:S(2)}, u32[]{:S(2)}) collective-permute-start(f32[2,2,4,1,256]{4,3,2,1,0:T(1,128)S(1)} %get-tuple-element.16), channel_id=1, source_target_pairs={{0,1},{1,2},{2,3},{3,4},{4,5},{5,6},{6,7},{8,9},{9,10},{10,11},{11... | collective-permute-start | bytes 49160 | tf_op jit(solution)/shard_map/ppermute | solution.py:14
  19.1 9.6 %collective-permute-start.7 = (f32[2,2,4,1,256]{4,3,2,1,0:T(1,128)S(1)}, f32[2,2,4,1,256]{4,3,2,1,0:T(1,128)S(1)}, u32[]{:S(2)}, u32[]{:S(2)}) collective-permute-start(f32[2,2,4,1,256]{4,3,2,1,0:T(1,128)S(1)} %get-tuple-element.17), channel_id=1, source_target_pairs={{1,0},{2,1},{3,2},{4,3},{5,4},{6,5},{7,6},{9,8},{10,9},{11,10},{12... | collective-permute-start | bytes 49160 | tf_op jit(solution)/shard_map/ppermute | solution.py:17
  23.6 5.1 %collective-permute-start.2 = (f32[32,4,1,256]{3,0,2,1:T(8,128)S(1)}, f32[32,4,1,256]{3,0,2,1:T(8,128)S(1)}, u32[]{:S(2)}, u32[]{:S(2)}) collective-permute-start(f32[32,4,1,256]{3,0,2,1:T(8,128)S(1)} %get-tuple-element.11), channel_id=1, source_target_pairs={{1,0},{2,1},{3,2},{4,3},{5,4},{6,5},{7,6},{9,8},{10,9},{11,10},{12... | collective-permute-start | bytes 393224 | tf_op jit(solution)/shard_map/ppermute | solution.py:17
  24.9 4.6 %collective-permute-start.3 = (f32[32,4,1,256]{3,0,2,1:T(8,128)S(1)}, f32[32,4,1,256]{3,0,2,1:T(8,128)S(1)}, u32[]{:S(2)}, u32[]{:S(2)}) collective-permute-start(f32[32,4,1,256]{3,0,2,1:T(8,128)S(1)} %get-tuple-element.10), channel_id=1, source_target_pairs={{0,1},{1,2},{2,3},{3,4},{4,5},{5,6},{6,7},{8,9},{9,10},{10,11},{11... | collective-permute-start | bytes 393224 | tf_op jit(solution)/shard_map/ppermute | solution.py:14
  48.8 6.9 %collective-permute-start.4 = (f32[32,4,1,256]{3,0,2,1:T(8,128)S(1)}, f32[32,4,1,256]{3,0,2,1:T(8,128)S(1)}, u32[]{:S(2)}, u32[]{:S(2)}) collective-permute-start(f32[32,4,1,256]{3,0,2,1:T(8,128)S(1)} %get-tuple-element.9), channel_id=1, source_target_pairs={{1,0},{2,1},{3,2},{4,3},{5,4},{6,5},{7,6},{9,8},{10,9},{11,10},{12... | collective-permute-start | bytes 393224 | tf_op jit(solution)/shard_map/ppermute | solution.py:17
  50.1 6.2 %collective-permute-start.5 = (f32[32,4,1,256]{3,0,2,1:T(8,128)S(1)}, f32[32,4,1,256]{3,0,2,1:T(8,128)S(1)}, u32[]{:S(2)}, u32[]{:S(2)}) collective-permute-start(f32[32,4,1,256]{3,0,2,1:T(8,128)S(1)} %get-tuple-element.8), channel_id=1, source_target_pairs={{0,1},{1,2},{2,3},{3,4},{4,5},{5,6},{6,7},{8,9},{9,10},{10,11},{11... | collective-permute-start | bytes 393224 | tf_op jit(solution)/shard_map/ppermute | solution.py:14
  59.7 7.4 %collective-permute-start.8 = (f32[32,4,1,256]{3,0,2,1:T(8,128)S(1)}, f32[32,4,1,256]{3,0,2,1:T(8,128)S(1)}, u32[]{:S(2)}, u32[]{:S(2)}) collective-permute-start(f32[32,4,1,256]{3,0,2,1:T(8,128)S(1)} %get-tuple-element.7), channel_id=1, source_target_pairs={{1,0},{2,1},{3,2},{4,3},{5,4},{6,5},{7,6},{9,8},{10,9},{11,10},{12... | collective-permute-start | bytes 393224 | tf_op jit(solution)/shard_map/ppermute | solution.py:17
  61.0 6.9 %collective-permute-start.9 = (f32[32,4,1,256]{3,0,2,1:T(8,128)S(1)}, f32[32,4,1,256]{3,0,2,1:T(8,128)S(1)}, u32[]{:S(2)}, u32[]{:S(2)}) collective-permute-start(f32[32,4,1,256]{3,0,2,1:T(8,128)S(1)} %get-tuple-element.6), channel_id=1, source_target_pairs={{0,1},{1,2},{2,3},{3,4},{4,5},{5,6},{6,7},{8,9},{9,10},{10,11},{11... | collective-permute-start | bytes 393224 | tf_op jit(solution)/shard_map/ppermute | solution.py:14
  72.8 1.6 copy-start
  113.6 50.0 %copy-start.1 = (f32[32,4096]{1,0:T(8,128)S(1)}, f32[32,4096]{1,0:T(8,128)}, u32[]{:S(2)}) copy-start(f32[32,4096]{1,0:T(8,128)} %reduce-scatter.2.cloned.1.call-done) | copy-start | bytes 1572868
  165.0 11.5 %all-to-all-start = ((f32[4,8,4096]{2,1,0:T(8,128)}), f32[4,8,4096]{2,1,0:T(8,128)S(1)}, u32[]{:S(2)}, u32[]{:S(2)}) async-start(f32[4,8,4096]{2,1,0:T(8,128)} %fusion), calls=%async_computation.1 | async-start | bytes 1048576 | tf_op jit(solution)/shard_map/all_to_all | solution.py:101
Sparse Core Ops, SparseCore 0:
  72.9 40.5 reduce-scatter.1
where the time goes:
time: 185 us; the launch traced here: 184 us
  waiting for transfers between devices  45.4 us (25%)
  blocking collectives  39.6 us (21%)
  starting transfers between devices  33.6 us (18%)
  other arithmetic  26.2 us (14%)
  local copies, waits for them, and re-layouts  19.5 us (11%)
  between operations  15 us (8%)
  matrix products  5.02 us (3%)
    psum x1, blocking collectives, on_device(): gram, cross = lax.psum((gram_part, cross_part), ('obs', 'space'))  39.6 us
    reduce_scatter x1, waiting for transfers between devices, on_device(): lax.psum_scatter(local_sketch, 'obs', scatter_dimension=1, tiled=True)  36.7 us
    ppermute x5, starting transfers between devices, extended_2(): lax.ppermute(lax.slice_in_dim(block, block.shape[dim] - width, None, axis...  22.6 us
    unnamed x14, local copies, waits for them, and re-layouts  8.66 us
    scatter-add x1, other arithmetic, on_device(): jnp.zeros_like(flat).at[:, cells].add(weighted).reshape(probes.shape)  7.01 us
    ppermute x5, starting transfers between devices, extended_2(): lax.ppermute(lax.slice_in_dim(block, 0, width, axis=dim), axis, backward)  6.46 us
    all_to_all x1, waiting for transfers between devices, on_device(): lax.all_to_all(basis_share, 'obs', split_axis=0, concat_axis=1, tiled=True)  6.45 us
    reshape x1, local copies, waits for them, and re-layouts, on_device(): jnp.zeros_like(flat).at[:, cells].add(weighted).reshape(probes.shape)  5.12 us
  transfers between devices with their start and end apart: 12, of which 5 were waited for; matrix products, arithmetic and copies ran while one was open for 3% of the time, Pallas kernels for 0%

commit v1 on v0

v1 whole, which is shorter than its diff:
```python
import functools
import math

import jax
import jax.numpy as jnp
from jax import lax
from jax.experimental import pallas as pl
from jax.experimental.pallas import tpu as pltpu
from jax.sharding import PartitionSpec as P

MESH = pl.DeviceIdType.MESH
REACH = 4
WIND_REACH = REACH - 1
HIGHEST = lax.Precision.HIGHEST


def dot_t(x, y):
    return lax.dot_general(
        x, y, (((1,), (1,)), ((), ())), precision=HIGHEST, preferred_element_type=jnp.float32
    )


def sketch_kernel(
    n, ns, rows, scale,
    probes_ref, rec_ref, out_ref, core_ref,
    ext, recx, slots, first, second, third, total, sums_o, sums_s, parts,
    local_sem, zsend, zrecv, wsend, wrecv, osend, orecv, ssend, srecv, bsend, brecv,
):
    levels, count, columns = ext.shape[1:]
    share = rows // n
    each = count // n
    me = lax.axis_index("obs")
    here = lax.axis_index("space")
    base = me * share
    has_low = here > 0
    has_high = here < ns - 1

    barrier = pltpu.get_barrier_semaphore()
    for j in range(1, n):
        pl.semaphore_signal(
            barrier, inc=1, device_id={"obs": lax.rem(me + j, n)}, device_id_type=MESH
        )
    for j in range(1, ns):
        pl.semaphore_signal(
            barrier, inc=1, device_id={"space": lax.rem(here + j, ns)}, device_id_type=MESH
        )
    load_rec = pltpu.make_async_copy(rec_ref, recx.at[pl.ds(WIND_REACH, rows)], local_sem.at[0])
    load_probes = pltpu.make_async_copy(probes_ref, ext.at[pl.ds(REACH, rows)], local_sem.at[1])
    load_rec.start()
    load_probes.start()

    @pl.when(jnp.logical_not(has_low))
    def _():
        recx[pl.ds(0, WIND_REACH)] = jnp.zeros((WIND_REACH,) + recx.shape[1:], jnp.float32)
        for r in range(REACH):
            ext[r] = jnp.zeros(ext.shape[1:], jnp.float32)

    @pl.when(jnp.logical_not(has_high))
    def _():
        recx[pl.ds(WIND_REACH + rows, WIND_REACH)] = jnp.zeros(
            (WIND_REACH,) + recx.shape[1:], jnp.float32
        )
        for r in range(REACH):
            ext[REACH + rows + r] = jnp.zeros(ext.shape[1:], jnp.float32)

    pl.semaphore_wait(barrier, n - 1 + ns - 1)

    up = {"space": lax.rem(here + 1, ns)}
    down = {"space": lax.rem(here + ns - 1, ns)}
    need_low = base < REACH
    need_high = (n - 1 - me) * share < REACH

    def z_copy(index, source, target, device):
        return pltpu.make_async_remote_copy(
            src_ref=source, dst_ref=target, send_sem=zsend.at[index], recv_sem=zrecv.at[index],
            device_id=device, device_id_type=MESH,
        )

    rec_up = z_copy(
        0, rec_ref.at[pl.ds(rows - WIND_REACH, WIND_REACH)], recx.at[pl.ds(0, WIND_REACH)], up
    )
    probes_up = z_copy(1, probes_ref.at[pl.ds(rows - REACH, REACH)], ext.at[pl.ds(0, REACH)], up)
    rec_down = z_copy(
        2, rec_ref.at[pl.ds(0, WIND_REACH)], recx.at[pl.ds(WIND_REACH + rows, WIND_REACH)], down
    )
    probes_down = z_copy(
        3, probes_ref.at[pl.ds(0, REACH)], ext.at[pl.ds(REACH + rows, REACH)], down
    )
    sends_up = jnp.logical_and(has_high, need_low)
    sends_down = jnp.logical_and(has_low, need_high)
    pl.when(has_high)(rec_up.start)
    pl.when(has_low)(rec_down.start)
    pl.when(sends_up)(probes_up.start)
    pl.when(sends_down)(probes_down.start)

    load_rec.wait()
    pl.when(has_low)(rec_up.wait_recv)
    pl.when(has_high)(rec_down.wait_recv)

    span = share + 2 * WIND_REACH

    def other(j):
        if n & (n - 1):
            return lax.rem(me + j, n)
        peer, bit = me, 1
        while bit < n:
            if j & bit:
                peer = peer + bit * (1 - 2 * lax.rem(me // bit, 2))
            bit *= 2
        return peer

    def w_copy(j):
        peer = other(j)
        slot = j if not n & (n - 1) else n - j
        return pltpu.make_async_remote_copy(
            src_ref=recx.at[pl.ds(peer * share, span)], dst_ref=slots.at[slot],
            send_sem=wsend.at[j], recv_sem=wrecv.at[slot],
            device_id={"obs": peer}, device_id_type=MESH,
        )

    own = pltpu.make_async_copy(recx.at[pl.ds(base, span)], slots.at[0], local_sem.at[2])
    own.start()
    winds = [w_copy(j) for j in range(1, n)]
    for copy in winds:
        copy.start()
    total[...] = jnp.zeros_like(total)
    own.wait()
    load_probes.wait()
    pl.when(jnp.logical_and(has_low, need_low))(probes_up.wait_recv)
    pl.when(jnp.logical_and(has_high, need_high))(probes_down.wait_recv)

    column = lax.broadcasted_iota(jnp.int32, (levels, columns), 1)
    inside_right = column < columns - 1
    inside_left = column > 0

    def valid(row):
        at = here * rows + row
        return jnp.where(jnp.logical_and(at >= 0, at < ns * rows), 1.0, 0.0).astype(jnp.float32)

    def wind_of(j, row, which):
        return slots[j, row, pl.ds(which * 8, 8), :][:levels]

    def advance(upper, centre, lower, cu, cd, cr, cl, keep, finish):
        cr = jnp.where(inside_right, cr, 0.0) * keep
        cl = jnp.where(inside_left, cl, 0.0) * keep
        cu = cu * keep
        cd = cd * keep
        mid = 0.2 * keep
        vertical = 0.1 * keep
        for lev in range(levels):
            u = centre[lev]
            if levels == 1:
                beside = jnp.zeros_like(u)
            elif lev == 0:
                beside = centre[1]
            elif lev == levels - 1:
                beside = centre[lev - 1]
            else:
                beside = centre[lev - 1] + centre[lev + 1]
            value = (
                mid * u
                + vertical * beside
                + cu[lev : lev + 1] * upper[lev]
                + cd[lev : lev + 1] * lower[lev]
                + cr[lev : lev + 1] * pltpu.roll(u, columns - 1, 1)
                + cl[lev : lev + 1] * pltpu.roll(u, 1, 1)
            )
            finish(lev, value)

    def window(j, carry):
        @pl.when(j > 0)
        def _():
            pltpu.make_async_remote_copy(
                src_ref=recx.at[pl.ds(0, span)], dst_ref=slots.at[j],
                send_sem=wsend.at[j], recv_sem=wrecv.at[j],
                device_id={"obs": lax.rem(me + 1, n)}, device_id_type=MESH,
            ).wait_recv()

        def forward_1(k, c):
            at = base + k + 1
            a, b = 0.5 * wind_of(j, k, 0), 0.5 * wind_of(j, k, 1)

            def finish(lev, value):
                first[k, lev] = value

            advance(
                ext.at[at + 1], ext.at[at], ext.at[at - 1],
                0.15 - a, 0.15 + a, 0.15 - b, 0.15 + b, valid(base + k - 3), finish,
            )
            return c

        def forward_2(k, c):
            a, b = 0.5 * wind_of(j, k + 1, 2), 0.5 * wind_of(j, k + 1, 3)
            weight = wind_of(j, k + 1, 4)

            def finish(lev, value):
                second[k, lev] = value * weight[lev : lev + 1]

            advance(
                first.at[k + 2], first.at[k + 1], first.at[k],
                0.15 - a, 0.15 + a, 0.15 - b, 0.15 + b, jnp.float32(1.0), finish,
            )
            return c

        def across(b):
            return 0.15 + pltpu.roll(b, columns - 1, 1), 0.15 - pltpu.roll(b, 1, 1)

        def adjoint_1(k, c):
            cr, cl = across(0.5 * wind_of(j, k + 2, 3))

            def finish(lev, value):
                third[k, lev] = value

            advance(
                second.at[k + 2], second.at[k + 1], second.at[k],
                0.15 + 0.5 * wind_of(j, k + 3, 2), 0.15 - 0.5 * wind_of(j, k + 1, 2),
                cr, cl, valid(base + k - 1), finish,
            )
            return c

        def adjoint_2(k, c):
            cr, cl = across(0.5 * wind_of(j, k + 3, 1))

            def finish(lev, value):
                total[k, lev] += value

            advance(
                third.at[k + 2], third.at[k + 1], third.at[k],
                0.15 + 0.5 * wind_of(j, k + 4, 0), 0.15 - 0.5 * wind_of(j, k + 2, 0),
                cr, cl, jnp.float32(1.0), finish,
            )
            return c

        lax.fori_loop(0, share + 6, forward_1, 0)
        lax.fori_loop(0, share + 4, forward_2, 0)
        lax.fori_loop(0, share + 2, adjoint_1, 0)
        lax.fori_loop(0, share, adjoint_2, 0)
        return carry

    lax.fori_loop(0, n, window, 0)

    products = jnp.zeros((count, 2 * count), jnp.float32)
    for k in range(share):
        for lev in range(levels):
            s = total[k, lev]
            both = jnp.concatenate([ext[base + REACH + k, lev], s], axis=0)
            products = products + dot_t(s, both)

    half = count // 2

    def summed(buffer, axis, size, index, send, recv, value):
        buffer[index] = value
        copies = []
        for j in range(1, size):
            peer = lax.rem(index + j, size)
            copies.append(
                pltpu.make_async_remote_copy(
                    src_ref=buffer.at[index], dst_ref=buffer.at[index],
                    send_sem=send.at[j], recv_sem=recv.at[j],
                    device_id={axis: peer}, device_id_type=MESH,
                )
            )
            copies[-1].start()
        for copy in copies:
            copy.wait()
        result = buffer[0]
        for j in range(1, size):
            result = result + buffer[j]
        return result

    packed = jnp.concatenate([products[:half], products[half:]], axis=1)
    packed = summed(sums_o, "obs", n, me, osend, orecv, packed)
    packed = summed(sums_s, "space", ns, here, ssend, srecv, packed)
    products = jnp.concatenate([packed[:, : 2 * count], packed[:, 2 * count :]], axis=0)
    core_ref[...] = products

    row_id = lax.broadcasted_iota(jnp.int32, (count, 2 * count), 0)
    lane_id = lax.broadcasted_iota(jnp.int32, (count, 2 * count), 1)
    work = jnp.where(lane_id < count, jnp.where(lane_id == row_id, 1.0, 0.0), products)
    for k in range(count):
        pivot = work[k : k + 1, :]
        root = lax.rsqrt(work[k : k + 1, count + k : count + k + 1])
        pivot = pivot * root
        factor = work[:, count + k : count + k + 1] * root
        work = jnp.where(
            row_id > k, work - factor * pivot, jnp.where(row_id == k, pivot, work)
        )
    inverse = work[:, :count] * scale

    copies = []
    for k in range(share):
        for lev in range(levels):
            block = jnp.dot(
                inverse, total[k, lev], precision=HIGHEST, preferred_element_type=jnp.float32
            )
            for p in range(n):
                parts[p, k, lev] = block[p * each : (p + 1) * each]
        for j in range(1, n):
            peer = other(j)
            copy = pltpu.make_async_remote_copy(
                src_ref=parts.at[peer, k], dst_ref=out_ref.at[base + k],
                send_sem=bsend.at[k, j], recv_sem=brecv.at[k, j],
                device_id={"obs": peer}, device_id_type=MESH,
            )
            copy.start()
            copies.append(copy)
        out_ref[base + k] = parts[me, k]

    for copy in copies:
        copy.wait()
    for copy in winds:
        copy.wait_send()
    pl.when(has_high)(rec_up.wait_send)
    pl.when(has_low)(rec_down.wait_send)
    pl.when(sends_up)(probes_up.wait_send)
    pl.when(sends_down)(probes_down.wait_send)


def on_device(probes, wind, station_cell, obs_count, obs_weight):
    count, levels, rows, columns = probes.shape
    n = lax.axis_size("obs")
    ns = lax.axis_size("space")
    slots = station_cell.shape[1]
    share = rows // n
    each = count // n

    live = lax.iota(jnp.int32, slots) < obs_count[0, 0]
    weight = jnp.where(live, obs_weight[0], 0.0)
    cells = station_cell[0]
    at_row = lax.broadcasted_iota(jnp.int32, (levels * rows, slots), 0) == (cells // columns)[None]
    at_column = lax.broadcasted_iota(jnp.int32, (columns, slots), 0) == (cells % columns)[None]
    weights = dot_t(
        jnp.where(at_row, weight[None], 0.0), at_column.astype(jnp.float32)
    ).reshape(levels, rows, columns)

    fields = [wind[0, 0, 0], wind[0, 0, 1], wind[0, 1, 0], wind[0, 1, 1], weights]
    record = jnp.stack(fields)
    record = jnp.pad(record, [(0, 0), (0, 8 - levels), (0, 0), (0, 0)])
    record = record.transpose(2, 0, 1, 3).reshape(rows, 8 * len(fields), columns)
    probes_t = probes.transpose(2, 1, 0, 3)

    depth = record.shape[1]
    f32 = jnp.float32
    dma = pltpu.SemaphoreType.DMA
    out, products = pl.pallas_call(
        functools.partial(sketch_kernel, n, ns, rows, math.sqrt(levels * rows * ns * columns)),
        out_shape=(
            jax.ShapeDtypeStruct((rows, levels, each, columns), f32),
            jax.ShapeDtypeStruct((count, 2 * count), f32),
        ),
        in_specs=[pl.BlockSpec(memory_space=pl.ANY)] * 2,
        out_specs=(
            pl.BlockSpec(memory_space=pltpu.VMEM),
            pl.BlockSpec(memory_space=pltpu.VMEM),
        ),
        scratch_shapes=[
            pltpu.VMEM((rows + 2 * REACH, levels, count, columns), f32),
            pltpu.VMEM((rows + 2 * WIND_REACH, depth, columns), f32),
            pltpu.VMEM((n, share + 2 * WIND_REACH, depth, columns), f32),
            pltpu.VMEM((share + 6, levels, count, columns), f32),
            pltpu.VMEM((share + 4, levels, count, columns), f32),
            pltpu.VMEM((share + 2, levels, count, columns), f32),
            pltpu.VMEM((share, levels, count, columns), f32),
            pltpu.VMEM((n, count // 2, 4 * count), f32),
            pltpu.VMEM((ns, count // 2, 4 * count), f32),
            pltpu.VMEM((n, share, levels, each, columns), f32),
            dma((3,)), dma((4,)), dma((4,)), dma((n,)), dma((n,)),
            dma((n,)), dma((n,)), dma((ns,)), dma((ns,)), dma((share, n)), dma((share, n)),
        ],
        compiler_params=pltpu.CompilerParams(
            collective_id=0, has_side_effects=True, vmem_limit_bytes=40 * 2**20
        ),
    )(probes_t, record)
    basis = out.transpose(2, 1, 0, 3)
    core = products[:, :count].T / (n * ns * slots)
    return basis, core


def solution(mesh):
    in_specs = (
        P(None, None, "space", None),
        P("obs", None, None, None, "space", None),
        P("obs", "space"),
        P("obs", "space"),
        P("obs", "space"),
    )
    out_specs = (P("obs", None, "space", None), P())
    return jax.shard_map(
        on_device, mesh=mesh, in_specs=in_specs, out_specs=out_specs, check_vma=False
    )
```

time: 185 us -> 62.5 us (0.34)
  Pallas kernels: 0 us -> 52.2 us
  waiting for transfers between devices: 45.4 us -> 0 us
  blocking collectives: 39.6 us -> 0 us
  starting transfers between devices: 33.6 us -> 0 us
  other arithmetic: 26.2 us -> 1.38 us
  between operations: 15 us -> 1.48 us
  local copies, waits for them, and re-layouts: 19.5 us -> 6.84 us
  matrix products: 5.02 us -> 0.28 us
    pallas_call x0 -> x1, Pallas kernels: none -> 52.2 us  [on_device(): pl.pallas_call(functools.partial(sketch_kernel, n, ns, rows, math.sqrt(le...]
    psum x1 -> x0, blocking collectives: 39.6 us -> none  [on_device(): gram, cross = lax.psum((gram_part, cross_part), ('obs', 'space'))]
    reduce_scatter x1 -> x0, waiting for transfers between devices: 36.7 us -> none  [on_device(): lax.psum_scatter(local_sketch, 'obs', scatter_dimension=1, tiled=True)]
    ppermute x10 -> x0, starting transfers between devices: 29.1 us -> none  [the longest x5 22.6 us: extended_2(): lax.ppermute(lax.slice_in_dim(block, block.shape[dim] - width, None, axis...]
    scatter-add x1 -> x0, other arithmetic: 7.01 us -> none  [on_device(): jnp.zeros_like(flat).at[:, cells].add(weighted).reshape(probes.shape)]
    another operation x5 -> x0, other arithmetic: 6.68 us -> none  [the longest x3 3.6 us: on_device(): lower = jnp.linalg.cholesky(gram)]
    all_to_all x1 -> x0, waiting for transfers between devices: 6.45 us -> none  [on_device(): lax.all_to_all(basis_share, 'obs', split_axis=0, concat_axis=1, tiled=True)]
    reshape x2 -> x0, local copies, waits for them, and re-layouts: 5.95 us -> none  [the longest x1 5.12 us: on_device(): jnp.zeros_like(flat).at[:, cells].add(weighted).reshape(probes.shape)]
  transfers between devices with their start and end apart: 12 -> 0, of which waited for: 5 -> 0; matrix products, arithmetic and copies ran while one was open for 3% -> 0% of each run, Pallas kernels for 0% -> 0%
where the time goes in v1:
time: 62.5 us; the launch traced here: 62.2 us
  Pallas kernels  52.2 us (84%)
  local copies, waits for them, and re-layouts  6.84 us (11%)
  between operations  1.48 us (2%)
  other arithmetic  1.38 us (2%)
    pallas_call x1, Pallas kernels, on_device(): pl.pallas_call(functools.partial(sketch_kernel, n, ns, rows, math.sqrt(le...  52.2 us
    unnamed x9, local copies, waits for them, and re-layouts  6.39 us

profile of v1, /device:TPU:0, one launch (start us, length us, event | category | flops | bytes accessed | tf_op | source)
XLA Modules:
  0.0 62.2 jit_solution(3186888035189435554)
XLA Ops:
  0.6 0.0 copy-start
  1.4 0.7 %compare_select_fusion = f32[1,256]{1,0:T(1,128)S(1)} fusion(f32[1,256]{1,0:T(1,128)} %param.9, s32[]{:T(128)} %bitcast.24), kind=kLoop, calls=%fused_computation.18 | loop fusion | flops 512 | bytes 2052 | tf_op jit(solution)/shard_map/jit(_where)/select_n | solution.py:328
  2.1 0.7 %and_select_fusion.1 = (s32[1,256]{1,0:T(1,128)S(1)}, s32[1,256]{1,0:T(1,128)S(1)}) fusion(s32[1,256]{1,0:T(1,128)} %param.7), kind=kLoop, calls=%fused_computation.19 | loop fusion | flops 3840 | bytes 3072 | tf_op jit(solution)/shard_map/jit(floor_divide)/jit(_where)/select_n | solution.py:330
  2.8 0.3 fusion
  3.1 0.8 %bitcast_dynamic-update-slice_fusion.3 = f32[5,4,16,256]{3,2,1,0:T(8,128)S(1)} fusion(f32[1,2,2,4,16,256]{5,4,3,2,1,0:T(8,128)} %param.6), kind=kLoop, calls=%fused_computation.9 | loop fusion | bytes 131072
  3.9 0.8 %bitcast_dynamic-update-slice_fusion.2 = f32[5,4,16,256]{3,2,1,0:T(8,128)S(1)} fusion(f32[5,4,16,256]{3,2,1,0:T(8,128)S(1)} %bitcast_dynamic-update-slice_fusion.3, f32[1,2,2,4,16,256]{5,4,3,2,1,0:T(8,128)} %param.6), kind=kLoop, calls=%fused_computation.8 | loop fusion | bytes 131072
  4.8 0.8 %bitcast_dynamic-update-slice_fusion.1 = f32[5,4,16,256]{3,2,1,0:T(8,128)S(1)} fusion(f32[5,4,16,256]{3,2,1,0:T(8,128)S(1)} %bitcast_dynamic-update-slice_fusion.2, f32[1,2,2,4,16,256]{5,4,3,2,1,0:T(8,128)} %param.6), kind=kLoop, calls=%fused_computation.7 | loop fusion | bytes 131072
  5.6 0.8 %bitcast_dynamic-update-slice_fusion = f32[5,4,16,256]{3,2,1,0:T(8,128)S(1)} fusion(f32[5,4,16,256]{3,2,1,0:T(8,128)S(1)} %bitcast_dynamic-update-slice_fusion.1, f32[1,2,2,4,16,256]{5,4,3,2,1,0:T(8,128)} %param.6), kind=kLoop, calls=%fused_computation.6 | loop fusion | bytes 131072
  6.5 0.1 pad_bitcast_fusion
  6.6 0.4 copy.14
  7.0 0.0 copy-done
  7.0 1.2 %copy.13 = f32[32,4,16,256]{3,0,1,2:T(8,128)S(1)} copy(f32[32,4,16,256]{3,2,1,0:T(8,128)S(1)} %copy-done) | data formatting | bytes 4194304 | tf_op args[0]
  8.2 52.2 %shard_map.68 = (f32[16,4,8,256]{3,2,1,0:T(8,128)S(1)}, f32[32,64]{1,0:T(8,128)S(1)}) custom-call(f32[16,4,32,256]{3,2,1,0:T(8,128)S(1)} %bitcast.25, f32[16,40,256]{2,1,0:T(8,128)S(1)} %bitcast.26), custom_call_target="tpu_custom_call" | custom-call | tf_op jit(solution)/shard_map/pallas_call | solution.py:345
  60.4 1.1 %copy.9 = f32[8,4,16,256]{3,2,1,0:T(8,128)} copy(f32[8,4,16,256]{3,0,1,2:T(8,128)S(1)} %bitcast.27) | data formatting | bytes 1048576
  61.5 0.7 %copy.10 = f32[32,32]{1,0:T(8,128)} copy(f32[32,32]{0,1:T(8,128)S(1)} %multiply_bitcast_fusion) | data formatting | bytes 8192
  (3 shorter events, 0.0 us)
Async XLA Ops:
  0.6 6.3 %copy-start = (f32[32,4,16,256]{3,2,1,0:T(8,128)S(1)}, f32[32,4,16,256]{3,2,1,0:T(8,128)}, u32[]{:S(2)}) copy-start(f32[32,4,16,256]{3,2,1,0:T(8,128)} %param.5) | copy-start | bytes 6291460

commit v2 on v1

--- a/solution.py
+++ b/solution.py
@@ -21,8 +21,8 @@
 
 
 def sketch_kernel(
-    n, ns, rows, scale,
-    probes_ref, rec_ref, out_ref, core_ref,
+    n, ns, rows, scale, divisor,
+    probes_ref, wind_ref, cells_ref, live_ref, weight_ref, out_ref, core_ref,
     ext, recx, slots, first, second, third, total, sums_o, sums_s, parts,
     local_sem, zsend, zrecv, wsend, wrecv, osend, orecv, ssend, srecv, bsend, brecv,
 ):
@@ -44,7 +44,10 @@
         pl.semaphore_signal(
             barrier, inc=1, device_id={"space": lax.rem(here + j, ns)}, device_id_type=MESH
         )
-    load_rec = pltpu.make_async_copy(rec_ref, recx.at[pl.ds(WIND_REACH, rows)], local_sem.at[0])
+    depth = wind_ref.shape[1]
+    load_rec = pltpu.make_async_copy(
+        wind_ref, recx.at[pl.ds(WIND_REACH, rows), pl.ds(0, depth)], local_sem.at[0]
+    )
     load_probes = pltpu.make_async_copy(probes_ref, ext.at[pl.ds(REACH, rows)], local_sem.at[1])
     load_rec.start()
     load_probes.start()
@@ -63,6 +66,24 @@
         for r in range(REACH):
             ext[REACH + rows + r] = jnp.zeros(ext.shape[1:], jnp.float32)
 
+    cells = cells_ref[...]
+    slot_count = cells.shape[1]
+    slot = lax.broadcasted_iota(jnp.int32, (1, slot_count), 1)
+    weight = jnp.where(slot < live_ref[0, 0], weight_ref[...], 0.0)
+    line = lax.broadcasted_iota(jnp.int32, (rows * levels, slot_count), 0)
+    start = (lax.rem(line, levels) * rows + lax.div(line, levels)) * columns
+    on_line = jnp.logical_and(cells >= start, cells < start + columns)
+    at_column = lax.rem(cells, columns) == lax.broadcasted_iota(
+        jnp.int32, (columns, slot_count), 0
+    )
+    weights = dot_t(
+        jnp.where(on_line, weight, 0.0), jnp.where(at_column, 1.0, 0.0).astype(jnp.float32)
+    )
+    for r in range(rows):
+        recx[WIND_REACH + r, pl.ds(depth, levels)] = weights[r * levels : (r + 1) * levels]
+    total[...] = jnp.zeros_like(total)
+    load_rec.wait()
+
     pl.semaphore_wait(barrier, n - 1 + ns - 1)
 
     up = {"space": lax.rem(here + 1, ns)}
@@ -77,23 +98,27 @@
         )
 
     rec_up = z_copy(
-        0, rec_ref.at[pl.ds(rows - WIND_REACH, WIND_REACH)], recx.at[pl.ds(0, WIND_REACH)], up
-    )
-    probes_up = z_copy(1, probes_ref.at[pl.ds(rows - REACH, REACH)], ext.at[pl.ds(0, REACH)], up)
+        0, recx.at[pl.ds(rows, WIND_REACH)], recx.at[pl.ds(0, WIND_REACH)], up
+    )
     rec_down = z_copy(
-        2, rec_ref.at[pl.ds(0, WIND_REACH)], recx.at[pl.ds(WIND_REACH + rows, WIND_REACH)], down
-    )
-    probes_down = z_copy(
-        3, probes_ref.at[pl.ds(0, REACH)], ext.at[pl.ds(REACH + rows, REACH)], down
-    )
+        1, recx.at[pl.ds(WIND_REACH, WIND_REACH)],
+        recx.at[pl.ds(WIND_REACH + rows, WIND_REACH)], down,
+    )
+    probes_up = [
+        z_copy(2 + h, probes_ref.at[rows - REACH + h], ext.at[h], up) for h in range(REACH)
+    ]
+    probes_down = [
+        z_copy(2 + REACH + h, probes_ref.at[h], ext.at[REACH + rows + h], down)
+        for h in range(REACH)
+    ]
     sends_up = jnp.logical_and(has_high, need_low)
     sends_down = jnp.logical_and(has_low, need_high)
     pl.when(has_high)(rec_up.start)
     pl.when(has_low)(rec_down.start)
-    pl.when(sends_up)(probes_up.start)
-    pl.when(sends_down)(probes_down.start)
-
-    load_rec.wait()
+    for copy in reversed(probes_up):
+        pl.when(sends_up)(copy.start)
+    for copy in probes_down:
+        pl.when(sends_down)(copy.start)
     pl.when(has_low)(rec_up.wait_recv)
     pl.when(has_high)(rec_down.wait_recv)
 
@@ -123,11 +148,10 @@
     winds = [w_copy(j) for j in range(1, n)]
     for copy in winds:
         copy.start()
-    total[...] = jnp.zeros_like(total)
     own.wait()
     load_probes.wait()
-    pl.when(jnp.logical_and(has_low, need_low))(probes_up.wait_recv)
-    pl.when(jnp.logical_and(has_high, need_high))(probes_down.wait_recv)
+    gets_low = jnp.logical_and(has_low, need_low)
+    gets_high = jnp.logical_and(has_high, need_high)
 
     column = lax.broadcasted_iota(jnp.int32, (levels, columns), 1)
     inside_right = column < columns - 1
@@ -138,7 +162,7 @@
         return jnp.where(jnp.logical_and(at >= 0, at < ns * rows), 1.0, 0.0).astype(jnp.float32)
 
     def wind_of(j, row, which):
-        return slots[j, row, pl.ds(which * 8, 8), :][:levels]
+        return slots[j, row, pl.ds(which * levels, levels), :]
 
     def advance(upper, centre, lower, cu, cd, cr, cl, keep, finish):
         cr = jnp.where(inside_right, cr, 0.0) * keep
@@ -167,6 +191,45 @@
             )
             finish(lev, value)
 
+    def forward_1(j, k):
+        at = base + k + 1
+        a, b = 0.5 * wind_of(j, k, 0), 0.5 * wind_of(j, k, 1)
+
+        def finish(lev, value):
+            first[k, lev] = value
+
+        advance(
+            ext.at[at + 1], ext.at[at], ext.at[at - 1],
+            0.15 - a, 0.15 + a, 0.15 - b, 0.15 + b, valid(base + k - 3), finish,
+        )
+
+    both_sides = jnp.logical_and(need_low, need_high)
+    for h in range(REACH):
+        pl.when(jnp.logical_and(gets_high, both_sides))(probes_down[h].wait_recv)
+
+    def arriving(i, c):
+        k = jnp.where(need_low, span - 1 - i, i)
+        for h in range(REACH):
+            pl.when(jnp.logical_and(gets_low, base + k == h))(probes_up[h].wait_recv)
+            pl.when(
+                jnp.logical_and(
+                    jnp.logical_and(gets_high, jnp.logical_not(both_sides)),
+                    base + k + 2 == REACH + rows + h,
+                )
+            )(probes_down[h].wait_recv)
+        forward_1(0, k)
+        return c
+
+    lax.fori_loop(0, span, arriving, 0)
+    for h in range(REACH):
+        pl.when(jnp.logical_and(gets_low, h < base))(probes_up[h].wait_recv)
+        pl.when(
+            jnp.logical_and(
+                jnp.logical_and(gets_high, jnp.logical_not(both_sides)),
+                base + span + 1 < REACH + rows + h,
+            )
+        )(probes_down[h].wait_recv)
+
     def window(j, carry):
         @pl.when(j > 0)
         def _():
@@ -176,18 +239,11 @@
                 device_id={"obs": lax.rem(me + 1, n)}, device_id_type=MESH,
             ).wait_recv()
 
-        def forward_1(k, c):
-            at = base + k + 1
-            a, b = 0.5 * wind_of(j, k, 0), 0.5 * wind_of(j, k, 1)
-
-            def finish(lev, value):
-                first[k, lev] = value
-
-            advance(
-                ext.at[at + 1], ext.at[at], ext.at[at - 1],
-                0.15 - a, 0.15 + a, 0.15 - b, 0.15 + b, valid(base + k - 3), finish,
-            )
-            return c
+            def step(k, c):
+                forward_1(j, k)
+                return c
+
+            lax.fori_loop(0, span, step, 0, unroll=2 if span % 2 == 0 else 1)
 
         def forward_2(k, c):
             a, b = 0.5 * wind_of(j, k + 1, 2), 0.5 * wind_of(j, k + 1, 3)
@@ -231,20 +287,20 @@
             )
             return c
 
-        lax.fori_loop(0, share + 6, forward_1, 0)
-        lax.fori_loop(0, share + 4, forward_2, 0)
-        lax.fori_loop(0, share + 2, adjoint_1, 0)
-        lax.fori_loop(0, share, adjoint_2, 0)
+        unroll = 2 if share % 2 == 0 else 1
+        lax.fori_loop(0, share + 4, forward_2, 0, unroll=unroll)
+        lax.fori_loop(0, share + 2, adjoint_1, 0, unroll=unroll)
+        lax.fori_loop(0, share, adjoint_2, 0, unroll=unroll)
         return carry
 
     lax.fori_loop(0, n, window, 0)
 
-    products = jnp.zeros((count, 2 * count), jnp.float32)
+    products = jnp.zeros((2 * count, count), jnp.float32)
     for k in range(share):
         for lev in range(levels):
             s = total[k, lev]
             both = jnp.concatenate([ext[base + REACH + k, lev], s], axis=0)
-            products = products + dot_t(s, both)
+            products = products + dot_t(both, s)
 
     half = count // 2
 
@@ -268,24 +324,24 @@
             result = result + buffer[j]
         return result
 
-    packed = jnp.concatenate([products[:half], products[half:]], axis=1)
+    packed = jnp.concatenate(
+        [products[i * half : (i + 1) * half] for i in (0, 2, 1, 3)], axis=1
+    )
     packed = summed(sums_o, "obs", n, me, osend, orecv, packed)
     packed = summed(sums_s, "space", ns, here, ssend, srecv, packed)
     products = jnp.concatenate([packed[:, : 2 * count], packed[:, 2 * count :]], axis=0)
-    core_ref[...] = products
+    core_ref[...] = products[:, :count] * (1.0 / divisor)
 
     row_id = lax.broadcasted_iota(jnp.int32, (count, 2 * count), 0)
     lane_id = lax.broadcasted_iota(jnp.int32, (count, 2 * count), 1)
     work = jnp.where(lane_id < count, jnp.where(lane_id == row_id, 1.0, 0.0), products)
-    for k in range(count):
+    for k in range(count - 1):
         pivot = work[k : k + 1, :]
-        root = lax.rsqrt(work[k : k + 1, count + k : count + k + 1])
-        pivot = pivot * root
-        factor = work[:, count + k : count + k + 1] * root
-        work = jnp.where(
-            row_id > k, work - factor * pivot, jnp.where(row_id == k, pivot, work)
-        )
-    inverse = work[:, :count] * scale
+        inverse = 1.0 / work[k : k + 1, count + k : count + k + 1]
+        factor = jnp.where(row_id > k, work[:, count + k : count + k + 1], 0.0)
+        work = work - (factor * pivot) * inverse
+    diagonal = jnp.sum(jnp.where(lane_id == row_id + count, work, 0.0), axis=1, keepdims=True)
+    inverse = work[:, :count] * (lax.rsqrt(diagonal) * scale)
 
     copies = []
     for k in range(share):
@@ -312,8 +368,10 @@
         copy.wait_send()
     pl.when(has_high)(rec_up.wait_send)
     pl.when(has_low)(rec_down.wait_send)
-    pl.when(sends_up)(probes_up.wait_send)
-    pl.when(sends_down)(probes_down.wait_send)
+    for copy in probes_up:
+        pl.when(sends_up)(copy.wait_send)
+    for copy in probes_down:
+        pl.when(sends_down)(copy.wait_send)
 
 
 def on_device(probes, wind, station_cell, obs_count, obs_weight):
@@ -324,31 +382,29 @@
     share = rows // n
     each = count // n
 
-    live = lax.iota(jnp.int32, slots) < obs_count[0, 0]
-    weight = jnp.where(live, obs_weight[0], 0.0)
-    cells = station_cell[0]
-    at_row = lax.broadcasted_iota(jnp.int32, (levels * rows, slots), 0) == (cells // columns)[None]
-    at_column = lax.broadcasted_iota(jnp.int32, (columns, slots), 0) == (cells % columns)[None]
-    weights = dot_t(
-        jnp.where(at_row, weight[None], 0.0), at_column.astype(jnp.float32)
-    ).reshape(levels, rows, columns)
-
-    fields = [wind[0, 0, 0], wind[0, 0, 1], wind[0, 1, 0], wind[0, 1, 1], weights]
-    record = jnp.stack(fields)
-    record = jnp.pad(record, [(0, 0), (0, 8 - levels), (0, 0), (0, 0)])
-    record = record.transpose(2, 0, 1, 3).reshape(rows, 8 * len(fields), columns)
+    steps, components = wind.shape[1:3]
+    lines = steps * components * levels
+    wind_t = wind[0].transpose(3, 0, 1, 2, 4).reshape(rows, lines, columns)
     probes_t = probes.transpose(2, 1, 0, 3)
-
-    depth = record.shape[1]
+    depth = lines + 8 * pl.cdiv(levels, 8)
+
     f32 = jnp.float32
     dma = pltpu.SemaphoreType.DMA
-    out, products = pl.pallas_call(
-        functools.partial(sketch_kernel, n, ns, rows, math.sqrt(levels * rows * ns * columns)),
+    out, core = pl.pallas_call(
+        functools.partial(
+            sketch_kernel, n, ns, rows, math.sqrt(levels * rows * ns * columns), n * ns * slots
+        ),
         out_shape=(
             jax.ShapeDtypeStruct((rows, levels, each, columns), f32),
-            jax.ShapeDtypeStruct((count, 2 * count), f32),
+            jax.ShapeDtypeStruct((count, count), f32),
         ),
-        in_specs=[pl.BlockSpec(memory_space=pl.ANY)] * 2,
+        in_specs=[
+            pl.BlockSpec(memory_space=pl.ANY),
+            pl.BlockSpec(memory_space=pl.ANY),
+            pl.BlockSpec(memory_space=pltpu.VMEM),
+            pl.BlockSpec(memory_space=pltpu.SMEM),
+            pl.BlockSpec(memory_space=pltpu.VMEM),
+        ],
         out_specs=(
             pl.BlockSpec(memory_space=pltpu.VMEM),
             pl.BlockSpec(memory_space=pltpu.VMEM),
@@ -364,15 +420,14 @@
             pltpu.VMEM((n, count // 2, 4 * count), f32),
             pltpu.VMEM((ns, count // 2, 4 * count), f32),
             pltpu.VMEM((n, share, levels, each, columns), f32),
-            dma((3,)), dma((4,)), dma((4,)), dma((n,)), dma((n,)),
+            dma((3,)), dma((2 + 2 * REACH,)), dma((2 + 2 * REACH,)), dma((n,)), dma((n,)),
             dma((n,)), dma((n,)), dma((ns,)), dma((ns,)), dma((share, n)), dma((share, n)),
         ],
         compiler_params=pltpu.CompilerParams(
             collective_id=0, has_side_effects=True, vmem_limit_bytes=40 * 2**20
         ),
-    )(probes_t, record)
+    )(probes_t, wind_t, station_cell, obs_count, obs_weight)
     basis = out.transpose(2, 1, 0, 3)
-    core = products[:, :count].T / (n * ns * slots)
     return basis, core
 
 

time: 62.5 us -> 53.2 us (0.85)
  Pallas kernels: 52.2 us -> 46 us
  other arithmetic: 1.38 us -> 0 us
  local copies, waits for them, and re-layouts: 6.84 us -> 5.64 us
    pallas_call x1, Pallas kernels: 52.2 us -> 46 us  [on_device(): pl.pallas_call(functools.partial(sketch_kernel, n, ns, rows, math.sqrt(le...]
    unnamed x9 -> x7, local copies, waits for them, and re-layouts: 6.39 us -> 4.54 us
    select_n x3 -> x0, other arithmetic: 1.38 us -> none  [the longest x1 0.69 us: on_device(): cells // columns]
    reshape x0 -> x1, local copies, waits for them, and re-layouts: none -> 1.11 us  [on_device(): wind_t = wind[0].transpose(3, 0, 1, 2, 4).reshape(rows, lines, columns)]
where the time goes in v2:
time: 53.2 us; the launch traced here: 53 us
  Pallas kernels  46 us (86%)
  local copies, waits for them, and re-layouts  5.64 us (11%)
  between operations  1.32 us (2%)
    pallas_call x1, Pallas kernels, on_device(): pl.pallas_call(functools.partial(sketch_kernel, n, ns, rows, math.sqrt(le...  46 us
    unnamed x7, local copies, waits for them, and re-layouts  4.54 us
    reshape x1, local copies, waits for them, and re-layouts, on_device(): wind_t = wind[0].transpose(3, 0, 1, 2, 4).reshape(rows, lines, columns)  1.11 us

profile of v2, /device:TPU:0, one launch (start us, length us, event | category | flops | bytes accessed | tf_op | source)
XLA Modules:
  0.0 53.0 jit_solution(9238699640197185663)
XLA Ops:
  1.3 1.1 %copy.10.wind_ref = f32[16,16,256]{2,1,0:T(8,128)S(1)} copy(f32[16,16,256]{2,0,1:T(8,128)} %bitcast.11) | data formatting | bytes 524288 | tf_op jit(solution)/shard_map/reshape | solution.py:387
  2.4 0.0 copy-start
  2.4 0.0 copy-start.1
  2.4 2.8 %copy.12 = f32[32,4,16,256]{3,0,1,2:T(8,128)S(1)} copy(f32[32,4,16,256]{3,2,1,0:T(8,128)} %param.5) | data formatting | bytes 4194304 | tf_op args[0]
  5.2 0.0 copy-done
  5.2 0.0 copy-done.1
  5.3 46.0 %shard_map.68 = (f32[16,4,8,256]{3,2,1,0:T(8,128)S(1)}, f32[32,32]{1,0:T(8,128)S(1)}) custom-call(f32[16,4,32,256]{3,2,1,0:T(8,128)S(1)} %bitcast.9, f32[16,16,256]{2,1,0:T(8,128)S(1)} %copy.10.wind_ref, s32[1,256]{1,0:T(1,128)S(1)} %copy-done, s32[1,1]{1,0:T(1,128)S(6)} %copy.14.live_ref, f32[1,256]{1,0:T(1,128)S(1)} %copy-done.1), custom_call_target="tpu_custom_call" | custom-call | tf_op jit(solution)/shard_map/pallas_call | solution.py:393
  51.3 1.1 %copy.9 = f32[8,4,16,256]{3,2,1,0:T(8,128)} copy(f32[8,4,16,256]{3,0,1,2:T(8,128)S(1)} %bitcast.10) | data formatting | bytes 1048576
  52.4 0.6 %copy.15 = f32[32,32]{1,0:T(8,128)} copy(f32[32,32]{1,0:T(8,128)S(1)} %get-tuple-element.11) | data formatting | bytes 8192
Async XLA Ops:
  2.4 2.8 %copy-start = (s32[1,256]{1,0:T(1,128)S(1)}, s32[1,256]{1,0:T(1,128)}, u32[]{:S(2)}) copy-start(s32[1,256]{1,0:T(1,128)} %cells_ref.1) | copy-start | bytes 3076
  2.4 2.8 %copy-start.1 = (f32[1,256]{1,0:T(1,128)S(1)}, f32[1,256]{1,0:T(1,128)}, u32[]{:S(2)}) copy-start(f32[1,256]{1,0:T(1,128)} %weight_ref.1) | copy-start | bytes 3076

commit v3 on v2

--- a/solution.py
+++ b/solution.py
@@ -24,7 +24,7 @@
     n, ns, rows, scale, divisor,
     probes_ref, wind_ref, cells_ref, live_ref, weight_ref, out_ref, core_ref,
     ext, recx, slots, first, second, third, total, sums_o, sums_s, parts,
-    local_sem, zsend, zrecv, wsend, wrecv, osend, orecv, ssend, srecv, bsend, brecv,
+    wind_raw, probes_raw, local_sem, zsend, zrecv, wsend, wrecv, osend, orecv, ssend, srecv, bsend, brecv,
 ):
     levels, count, columns = ext.shape[1:]
     share = rows // n
@@ -44,12 +44,12 @@
         pl.semaphore_signal(
             barrier, inc=1, device_id={"space": lax.rem(here + j, ns)}, device_id_type=MESH
         )
-    depth = wind_ref.shape[1]
-    load_rec = pltpu.make_async_copy(
-        wind_ref, recx.at[pl.ds(WIND_REACH, rows), pl.ds(0, depth)], local_sem.at[0]
-    )
-    load_probes = pltpu.make_async_copy(probes_ref, ext.at[pl.ds(REACH, rows)], local_sem.at[1])
-    load_rec.start()
+    depth = wind_ref.shape[0]
+    need_low = base < REACH
+    need_high = (n - 1 - me) * share < REACH
+    load_winds = pltpu.make_async_copy(wind_ref, wind_raw, local_sem.at[0])
+    load_probes = pltpu.make_async_copy(probes_ref, probes_raw, local_sem.at[1])
+    load_winds.start()
     load_probes.start()
 
     @pl.when(jnp.logical_not(has_low))
@@ -82,14 +82,13 @@
     for r in range(rows):
         recx[WIND_REACH + r, pl.ds(depth, levels)] = weights[r * levels : (r + 1) * levels]
     total[...] = jnp.zeros_like(total)
-    load_rec.wait()
+    load_winds.wait()
+    recx[pl.ds(WIND_REACH, rows), pl.ds(0, depth)] = jnp.swapaxes(wind_raw[...], 0, 1)
 
     pl.semaphore_wait(barrier, n - 1 + ns - 1)
 
     up = {"space": lax.rem(here + 1, ns)}
     down = {"space": lax.rem(here + ns - 1, ns)}
-    need_low = base < REACH
-    need_high = (n - 1 - me) * share < REACH
 
     def z_copy(index, source, target, device):
         return pltpu.make_async_remote_copy(
@@ -105,22 +104,23 @@
         recx.at[pl.ds(WIND_REACH + rows, WIND_REACH)], down,
     )
     probes_up = [
-        z_copy(2 + h, probes_ref.at[rows - REACH + h], ext.at[h], up) for h in range(REACH)
+        z_copy(2 + h, ext.at[rows + h], ext.at[h], up) for h in range(REACH)
     ]
     probes_down = [
-        z_copy(2 + REACH + h, probes_ref.at[h], ext.at[REACH + rows + h], down)
+        z_copy(2 + REACH + h, ext.at[REACH + h], ext.at[REACH + rows + h], down)
         for h in range(REACH)
     ]
     sends_up = jnp.logical_and(has_high, need_low)
     sends_down = jnp.logical_and(has_low, need_high)
     pl.when(has_high)(rec_up.start)
     pl.when(has_low)(rec_down.start)
+    load_probes.wait()
+    for lev in range(levels):
+        ext[pl.ds(REACH, rows), lev] = jnp.swapaxes(probes_raw[:, lev], 0, 1)
     for copy in reversed(probes_up):
         pl.when(sends_up)(copy.start)
     for copy in probes_down:
         pl.when(sends_down)(copy.start)
-    pl.when(has_low)(rec_up.wait_recv)
-    pl.when(has_high)(rec_down.wait_recv)
 
     span = share + 2 * WIND_REACH
 
@@ -143,13 +143,6 @@
             device_id={"obs": peer}, device_id_type=MESH,
         )
 
-    own = pltpu.make_async_copy(recx.at[pl.ds(base, span)], slots.at[0], local_sem.at[2])
-    own.start()
-    winds = [w_copy(j) for j in range(1, n)]
-    for copy in winds:
-        copy.start()
-    own.wait()
-    load_probes.wait()
     gets_low = jnp.logical_and(has_low, need_low)
     gets_high = jnp.logical_and(has_high, need_high)
 
@@ -161,8 +154,11 @@
         at = here * rows + row
         return jnp.where(jnp.logical_and(at >= 0, at < ns * rows), 1.0, 0.0).astype(jnp.float32)
 
-    def wind_of(j, row, which):
-        return slots[j, row, pl.ds(which * levels, levels), :]
+    def own_wind(row, which):
+        return recx[base + row, pl.ds(which * levels, levels), :]
+
+    def wind_in(j):
+        return lambda row, which: slots[j, row, pl.ds(which * levels, levels), :]
 
     def advance(upper, centre, lower, cu, cd, cr, cl, keep, finish):
         cr = jnp.where(inside_right, cr, 0.0) * keep
@@ -191,9 +187,9 @@
             )
             finish(lev, value)
 
-    def forward_1(j, k):
+    def forward_1(wind_of, k):
         at = base + k + 1
-        a, b = 0.5 * wind_of(j, k, 0), 0.5 * wind_of(j, k, 1)
+        a, b = 0.5 * wind_of(k, 0), 0.5 * wind_of(k, 1)
 
         def finish(lev, value):
             first[k, lev] = value
@@ -203,12 +199,76 @@
             0.15 - a, 0.15 + a, 0.15 - b, 0.15 + b, valid(base + k - 3), finish,
         )
 
+    def forward_2(wind_of, k):
+        a, b = 0.5 * wind_of(k + 1, 2), 0.5 * wind_of(k + 1, 3)
+        weight = wind_of(k + 1, 4)
+
+        def finish(lev, value):
+            second[k, lev] = value * weight[lev : lev + 1]
+
+        advance(
+            first.at[k + 2], first.at[k + 1], first.at[k],
+            0.15 - a, 0.15 + a, 0.15 - b, 0.15 + b, jnp.float32(1.0), finish,
+        )
+
+    def across(b):
+        return 0.15 + pltpu.roll(b, columns - 1, 1), 0.15 - pltpu.roll(b, 1, 1)
+
+    def adjoint_1(wind_of, k):
+        cr, cl = across(0.5 * wind_of(k + 2, 3))
+
+        def finish(lev, value):
+            third[k, lev] = value
+
+        advance(
+            second.at[k + 2], second.at[k + 1], second.at[k],
+            0.15 + 0.5 * wind_of(k + 3, 2), 0.15 - 0.5 * wind_of(k + 1, 2),
+            cr, cl, valid(base + k - 1), finish,
+        )
+
+    def adjoint_2(wind_of, k):
+        cr, cl = across(0.5 * wind_of(k + 3, 1))
+
+        def finish(lev, value):
+            total[k, lev] += value
+
+        advance(
+            third.at[k + 2], third.at[k + 1], third.at[k],
+            0.15 + 0.5 * wind_of(k + 4, 0), 0.15 - 0.5 * wind_of(k + 2, 0),
+            cr, cl, jnp.float32(1.0), finish,
+        )
+
     both_sides = jnp.logical_and(need_low, need_high)
-    for h in range(REACH):
-        pl.when(jnp.logical_and(gets_high, both_sides))(probes_down[h].wait_recv)
+    ready = span
+    for at in (p * share for p in range(n)):
+        if at < REACH:
+            ready = min(ready, span - (REACH - at))
+        if (n - 1) * share - at < REACH:
+            ready = min(ready, REACH + rows - 2 - at)
+    wavefront = ready >= 6
+
+    def place(i, stage):
+        return jnp.where(need_low, span - 1 - i, i - 2 * stage)
+
+    unroll = 2 if share % 2 == 0 else 1
+    later = ((2, forward_2), (4, adjoint_1), (6, adjoint_2))
+
+    def local_row(i, c):
+        forward_1(own_wind, place(i, 0))
+        return c
+
+    def later_sweeps(end):
+        for begin, step in later:
+
+            def body(i, c):
+                step(own_wind, place(i, begin // 2))
+                return c
+
+            if begin < end:
+                lax.fori_loop(begin, end, body, 0, unroll=unroll)
 
     def arriving(i, c):
-        k = jnp.where(need_low, span - 1 - i, i)
+        k = place(i, 0)
         for h in range(REACH):
             pl.when(jnp.logical_and(gets_low, base + k == h))(probes_up[h].wait_recv)
             pl.when(
@@ -217,10 +277,26 @@
                     base + k + 2 == REACH + rows + h,
                 )
             )(probes_down[h].wait_recv)
-        forward_1(0, k)
+        forward_1(own_wind, k)
+        if wavefront:
+            for begin, step in later:
+                step(own_wind, place(i, begin // 2))
         return c
 
-    lax.fori_loop(0, span, arriving, 0)
+    if wavefront:
+        lax.fori_loop(0, ready, local_row, 0, unroll=unroll)
+
+    pl.when(has_low)(rec_up.wait_recv)
+    pl.when(has_high)(rec_down.wait_recv)
+    winds = [w_copy(j) for j in range(1, n)]
+    for copy in winds:
+        copy.start()
+
+    if wavefront:
+        later_sweeps(ready)
+    for h in range(REACH):
+        pl.when(jnp.logical_and(gets_high, both_sides))(probes_down[h].wait_recv)
+    lax.fori_loop(ready if wavefront else 0, span, arriving, 0)
     for h in range(REACH):
         pl.when(jnp.logical_and(gets_low, h < base))(probes_up[h].wait_recv)
         pl.when(
@@ -230,70 +306,30 @@
             )
         )(probes_down[h].wait_recv)
 
+    if not wavefront:
+        later_sweeps(span)
+
     def window(j, carry):
-        @pl.when(j > 0)
-        def _():
-            pltpu.make_async_remote_copy(
-                src_ref=recx.at[pl.ds(0, span)], dst_ref=slots.at[j],
-                send_sem=wsend.at[j], recv_sem=wrecv.at[j],
-                device_id={"obs": lax.rem(me + 1, n)}, device_id_type=MESH,
-            ).wait_recv()
-
-            def step(k, c):
-                forward_1(j, k)
+        pltpu.make_async_remote_copy(
+            src_ref=recx.at[pl.ds(0, span)], dst_ref=slots.at[j],
+            send_sem=wsend.at[j], recv_sem=wrecv.at[j],
+            device_id={"obs": lax.rem(me + 1, n)}, device_id_type=MESH,
+        ).wait_recv()
+
+        def sweep(step, length):
+            def body(k, c):
+                step(wind_in(j), k)
                 return c
 
-            lax.fori_loop(0, span, step, 0, unroll=2 if span % 2 == 0 else 1)
-
-        def forward_2(k, c):
-            a, b = 0.5 * wind_of(j, k + 1, 2), 0.5 * wind_of(j, k + 1, 3)
-            weight = wind_of(j, k + 1, 4)
-
-            def finish(lev, value):
-                second[k, lev] = value * weight[lev : lev + 1]
-
-            advance(
-                first.at[k + 2], first.at[k + 1], first.at[k],
-                0.15 - a, 0.15 + a, 0.15 - b, 0.15 + b, jnp.float32(1.0), finish,
-            )
-            return c
-
-        def across(b):
-            return 0.15 + pltpu.roll(b, columns - 1, 1), 0.15 - pltpu.roll(b, 1, 1)
-
-        def adjoint_1(k, c):
-            cr, cl = across(0.5 * wind_of(j, k + 2, 3))
-
-            def finish(lev, value):
-                third[k, lev] = value
-
-            advance(
-                second.at[k + 2], second.at[k + 1], second.at[k],
-                0.15 + 0.5 * wind_of(j, k + 3, 2), 0.15 - 0.5 * wind_of(j, k + 1, 2),
-                cr, cl, valid(base + k - 1), finish,
-            )
-            return c
-
-        def adjoint_2(k, c):
-            cr, cl = across(0.5 * wind_of(j, k + 3, 1))
-
-            def finish(lev, value):
-                total[k, lev] += value
-
-            advance(
-                third.at[k + 2], third.at[k + 1], third.at[k],
-                0.15 + 0.5 * wind_of(j, k + 4, 0), 0.15 - 0.5 * wind_of(j, k + 2, 0),
-                cr, cl, jnp.float32(1.0), finish,
-            )
-            return c
-
-        unroll = 2 if share % 2 == 0 else 1
-        lax.fori_loop(0, share + 4, forward_2, 0, unroll=unroll)
-        lax.fori_loop(0, share + 2, adjoint_1, 0, unroll=unroll)
-        lax.fori_loop(0, share, adjoint_2, 0, unroll=unroll)
+            lax.fori_loop(0, length, body, 0, unroll=unroll)
+
+        sweep(forward_1, share + 6)
+        sweep(forward_2, share + 4)
+        sweep(adjoint_1, share + 2)
+        sweep(adjoint_2, share)
         return carry
 
-    lax.fori_loop(0, n, window, 0)
+    lax.fori_loop(1, n, window, 0)
 
     products = jnp.zeros((2 * count, count), jnp.float32)
     for k in range(share):
@@ -384,8 +420,7 @@
 
     steps, components = wind.shape[1:3]
     lines = steps * components * levels
-    wind_t = wind[0].transpose(3, 0, 1, 2, 4).reshape(rows, lines, columns)
-    probes_t = probes.transpose(2, 1, 0, 3)
+    winds = wind.reshape(lines, rows, columns)
     depth = lines + 8 * pl.cdiv(levels, 8)
 
     f32 = jnp.float32
@@ -399,8 +434,8 @@
             jax.ShapeDtypeStruct((count, count), f32),
         ),
         in_specs=[
-            pl.BlockSpec(memory_space=pl.ANY),
-            pl.BlockSpec(memory_space=pl.ANY),
+            pl.BlockSpec(memory_space=pltpu.HBM),
+            pl.BlockSpec(memory_space=pltpu.HBM),
             pl.BlockSpec(memory_space=pltpu.VMEM),
             pl.BlockSpec(memory_space=pltpu.SMEM),
             pl.BlockSpec(memory_space=pltpu.VMEM),
@@ -420,13 +455,15 @@
             pltpu.VMEM((n, count // 2, 4 * count), f32),
             pltpu.VMEM((ns, count // 2, 4 * count), f32),
             pltpu.VMEM((n, share, levels, each, columns), f32),
-            dma((3,)), dma((2 + 2 * REACH,)), dma((2 + 2 * REACH,)), dma((n,)), dma((n,)),
+            pltpu.VMEM((lines, rows, columns), f32),
+            pltpu.VMEM((count, levels, rows, columns), f32),
+            dma((2,)), dma((2 + 2 * REACH,)), dma((2 + 2 * REACH,)), dma((n,)), dma((n,)),
             dma((n,)), dma((n,)), dma((ns,)), dma((ns,)), dma((share, n)), dma((share, n)),
         ],
         compiler_params=pltpu.CompilerParams(
             collective_id=0, has_side_effects=True, vmem_limit_bytes=40 * 2**20
         ),
-    )(probes_t, wind_t, station_cell, obs_count, obs_weight)
+    )(probes, winds, station_cell, obs_count, obs_weight)
     basis = out.transpose(2, 1, 0, 3)
     return basis, core
 

time: 53.2 us -> 52.8 us (level)
    reshape x1 -> x0, local copies, waits for them, and re-layouts: 1.11 us -> none  [on_device(): wind_t = wind[0].transpose(3, 0, 1, 2, 4).reshape(rows, lines, columns)]
    unnamed x7 -> x10, local copies, waits for them, and re-layouts: 4.54 us -> 5.6 us
where the time goes in v3:
time: 52.8 us; the launch traced here: 52.5 us
  Pallas kernels  45.6 us (86%)
  local copies, waits for them, and re-layouts  5.6 us (11%)
  between operations  1.3 us (2%)
    pallas_call x1, Pallas kernels, on_device(): pl.pallas_call(functools.partial(sketch_kernel, n, ns, rows, math.sqrt(le...  45.6 us
    unnamed x10, local copies, waits for them, and re-layouts  5.6 us

profile of v3, /device:TPU:0, one launch (start us, length us, event | category | flops | bytes accessed | tf_op | source)
XLA Modules:
  0.0 52.5 jit_solution(9685320308905669505)
XLA Ops:
  1.3 0.0 copy-start
  1.3 1.6 %copy-done = f32[32,4,16,256]{3,2,1,0:T(8,128)S(1)} copy-done((f32[32,4,16,256]{3,2,1,0:T(8,128)S(1)}, f32[32,4,16,256]{3,2,1,0:T(8,128)}, u32[]{:S(2)}) %copy-start) | copy-done | bytes 2097176
  2.9 0.0 copy-start.1
  2.9 0.9 %copy-done.1 = f32[1,2,2,4,16,256]{5,4,3,2,1,0:T(8,128)S(1)} copy-done((f32[1,2,2,4,16,256]{5,4,3,2,1,0:T(8,128)S(1)}, f32[1,2,2,4,16,256]{5,4,3,2,1,0:T(8,128)}, u32[]{:S(2)}) %copy-start.1) | copy-done | bytes 262168
  3.8 0.0 copy-start.2
  3.8 0.7 %copy-done.2 = s32[1,256]{1,0:T(1,128)S(1)} copy-done((s32[1,256]{1,0:T(1,128)S(1)}, s32[1,256]{1,0:T(1,128)}, u32[]{:S(2)}) %copy-start.2) | copy-done | bytes 1048
  4.5 0.0 copy-start.3
  4.5 0.7 %copy-done.3 = f32[1,256]{1,0:T(1,128)S(1)} copy-done((f32[1,256]{1,0:T(1,128)S(1)}, f32[1,256]{1,0:T(1,128)}, u32[]{:S(2)}) %copy-start.3) | copy-done | bytes 1048
  5.2 45.6 %shard_map.68 = (f32[16,4,8,256]{3,2,1,0:T(8,128)S(1)}, f32[32,32]{1,0:T(8,128)S(1)}) custom-call(f32[32,4,16,256]{3,2,1,0:T(8,128)S(1)} %copy-done, f32[16,16,256]{2,1,0:T(8,128)S(1)} %bitcast.3, s32[1,256]{1,0:T(1,128)S(1)} %copy-done.2, s32[1,1]{1,0:T(1,128)S(6)} %copy.9.live_ref, f32[1,256]{1,0:T(1,128)S(1)} %copy-done.3), custom_call_target="tpu_custom_call" | custom-call | tf_op jit(solution)/shard_map/pallas_call | solution.py:428
  50.8 1.1 %copy.7 = f32[8,4,16,256]{3,2,1,0:T(8,128)} copy(f32[8,4,16,256]{3,0,1,2:T(8,128)S(1)} %bitcast.2) | data formatting | bytes 1048576
  51.9 0.6 %copy.10 = f32[32,32]{1,0:T(8,128)} copy(f32[32,32]{1,0:T(8,128)S(1)} %get-tuple-element.11) | data formatting | bytes 8192
Async XLA Ops:
  1.3 1.6 %copy-start = (f32[32,4,16,256]{3,2,1,0:T(8,128)S(1)}, f32[32,4,16,256]{3,2,1,0:T(8,128)}, u32[]{:S(2)}) copy-start(f32[32,4,16,256]{3,2,1,0:T(8,128)} %probes_ref.1) | copy-start | bytes 6291460
  2.9 0.9 %copy-start.1 = (f32[1,2,2,4,16,256]{5,4,3,2,1,0:T(8,128)S(1)}, f32[1,2,2,4,16,256]{5,4,3,2,1,0:T(8,128)}, u32[]{:S(2)}) copy-start(f32[1,2,2,4,16,256]{5,4,3,2,1,0:T(8,128)} %param.6) | copy-start | bytes 786436
  3.8 0.7 %copy-start.2 = (s32[1,256]{1,0:T(1,128)S(1)}, s32[1,256]{1,0:T(1,128)}, u32[]{:S(2)}) copy-start(s32[1,256]{1,0:T(1,128)} %cells_ref.1) | copy-start | bytes 3076
  4.5 0.7 %copy-start.3 = (f32[1,256]{1,0:T(1,128)S(1)}, f32[1,256]{1,0:T(1,128)}, u32[]{:S(2)}) copy-start(f32[1,256]{1,0:T(1,128)} %weight_ref.1) | copy-start | bytes 3076

commit v4 on v3

--- a/solution.py
+++ b/solution.py
@@ -11,6 +11,7 @@
 MESH = pl.DeviceIdType.MESH
 REACH = 4
 WIND_REACH = REACH - 1
+VMEM_BYTES = 64 * 2**20
 HIGHEST = lax.Precision.HIGHEST
 
 
@@ -24,7 +25,7 @@
     n, ns, rows, scale, divisor,
     probes_ref, wind_ref, cells_ref, live_ref, weight_ref, out_ref, core_ref,
     ext, recx, slots, first, second, third, total, sums_o, sums_s, parts,
-    wind_raw, probes_raw, local_sem, zsend, zrecv, wsend, wrecv, osend, orecv, ssend, srecv, bsend, brecv,
+    wind_raw, probes_raw, cells_raw, weight_raw, local_sem, zsend, zrecv, wsend, wrecv, osend, orecv, ssend, srecv, bsend, brecv,
 ):
     levels, count, columns = ext.shape[1:]
     share = rows // n
@@ -49,8 +50,10 @@
     need_high = (n - 1 - me) * share < REACH
     load_winds = pltpu.make_async_copy(wind_ref, wind_raw, local_sem.at[0])
     load_probes = pltpu.make_async_copy(probes_ref, probes_raw, local_sem.at[1])
-    load_winds.start()
-    load_probes.start()
+    load_cells = pltpu.make_async_copy(cells_ref, cells_raw, local_sem.at[2])
+    load_weight = pltpu.make_async_copy(weight_ref, weight_raw, local_sem.at[3])
+    for load in (load_cells, load_weight, load_winds, load_probes):
+        load.start()
 
     @pl.when(jnp.logical_not(has_low))
     def _():
@@ -66,10 +69,12 @@
         for r in range(REACH):
             ext[REACH + rows + r] = jnp.zeros(ext.shape[1:], jnp.float32)
 
-    cells = cells_ref[...]
+    load_cells.wait()
+    load_weight.wait()
+    cells = cells_raw[...]
     slot_count = cells.shape[1]
     slot = lax.broadcasted_iota(jnp.int32, (1, slot_count), 1)
-    weight = jnp.where(slot < live_ref[0, 0], weight_ref[...], 0.0)
+    weight = jnp.where(slot < live_ref[0, 0], weight_raw[...], 0.0)
     line = lax.broadcasted_iota(jnp.int32, (rows * levels, slot_count), 0)
     start = (lax.rem(line, levels) * rows + lax.div(line, levels)) * columns
     on_line = jnp.logical_and(cells >= start, cells < start + columns)
@@ -434,11 +439,11 @@
             jax.ShapeDtypeStruct((count, count), f32),
         ),
         in_specs=[
-            pl.BlockSpec(memory_space=pltpu.HBM),
-            pl.BlockSpec(memory_space=pltpu.HBM),
-            pl.BlockSpec(memory_space=pltpu.VMEM),
+            pl.BlockSpec(memory_space=pl.ANY),
+            pl.BlockSpec(memory_space=pl.ANY),
+            pl.BlockSpec(memory_space=pl.ANY),
             pl.BlockSpec(memory_space=pltpu.SMEM),
-            pl.BlockSpec(memory_space=pltpu.VMEM),
+            pl.BlockSpec(memory_space=pl.ANY),
         ],
         out_specs=(
             pl.BlockSpec(memory_space=pltpu.VMEM),
@@ -457,11 +462,13 @@
             pltpu.VMEM((n, share, levels, each, columns), f32),
             pltpu.VMEM((lines, rows, columns), f32),
             pltpu.VMEM((count, levels, rows, columns), f32),
-            dma((2,)), dma((2 + 2 * REACH,)), dma((2 + 2 * REACH,)), dma((n,)), dma((n,)),
+            pltpu.VMEM((1, slots), jnp.int32),
+            pltpu.VMEM((1, slots), f32),
+            dma((4,)), dma((2 + 2 * REACH,)), dma((2 + 2 * REACH,)), dma((n,)), dma((n,)),
             dma((n,)), dma((n,)), dma((ns,)), dma((ns,)), dma((share, n)), dma((share, n)),
         ],
         compiler_params=pltpu.CompilerParams(
-            collective_id=0, has_side_effects=True, vmem_limit_bytes=40 * 2**20
+            collective_id=0, has_side_effects=True, vmem_limit_bytes=VMEM_BYTES
         ),
     )(probes, winds, station_cell, obs_count, obs_weight)
     basis = out.transpose(2, 1, 0, 3)

time: 52.8 us -> 51.5 us (0.975)
  local copies, waits for them, and re-layouts: 5.6 us -> 3.47 us
  Pallas kernels: 45.6 us -> 46.5 us
    unnamed x10 -> x2, local copies, waits for them, and re-layouts: 5.6 us -> 3.47 us
    pallas_call x1, Pallas kernels: 45.6 us -> 46.5 us  [on_device(): pl.pallas_call(functools.partial(sketch_kernel, n, ns, rows, math.sqrt(le...]
where the time goes in v4:
time: 51.5 us; the launch traced here: 51.3 us
  Pallas kernels  46.5 us (90%)
  local copies, waits for them, and re-layouts  3.47 us (7%)
  between operations  1.29 us (3%)
    pallas_call x1, Pallas kernels, on_device(): pl.pallas_call(functools.partial(sketch_kernel, n, ns, rows, math.sqrt(le...  46.5 us
    unnamed x2, local copies, waits for them, and re-layouts  3.47 us

profile of v4, /device:TPU:0, one launch (start us, length us, event | category | flops | bytes accessed | tf_op | source)
XLA Modules:
  0.0 51.3 jit_solution(4639318018587468959)
XLA Ops:
  1.3 46.5 %shard_map.68 = (f32[16,4,8,256]{3,2,1,0:T(8,128)}, f32[32,32]{1,0:T(8,128)}) custom-call(f32[32,4,16,256]{3,2,1,0:T(8,128)} %probes_ref.1, f32[16,16,256]{2,1,0:T(8,128)} %bitcast.3, s32[1,256]{1,0:T(1,128)} %cells_ref.1, s32[1,1]{1,0:T(1,128)S(6)} %copy.9.live_ref, f32[1,256]{1,0:T(1,128)} %weight_ref.1), custom_call_target="tpu_custom_call" | custom-call | tf_op jit(solution)/shard_map/pallas_call | solution.py:433
  47.8 2.1 %copy.7 = f32[8,4,16,256]{3,2,1,0:T(8,128)} copy(f32[8,4,16,256]{3,0,1,2:T(8,128)} %bitcast.2) | data formatting | bytes 1048576
  49.9 1.3 %copy.10 = f32[32,32]{1,0:T(8,128)} copy(f32[32,32]{1,0:T(8,128)} %get-tuple-element.11) | data formatting | bytes 8192

commit v5 on v4

--- a/solution.py
+++ b/solution.py
@@ -19,6 +19,14 @@
     return lax.dot_general(
         x, y, (((1,), (1,)), ((), ())), precision=HIGHEST, preferred_element_type=jnp.float32
     )
+
+
+def split(x):
+    high = x.astype(jnp.bfloat16)
+    rest = x - high.astype(jnp.float32)
+    middle = rest.astype(jnp.bfloat16)
+    low = (rest - middle.astype(jnp.float32)).astype(jnp.bfloat16)
+    return high, middle, low
 
 
 def sketch_kernel(
@@ -339,9 +347,19 @@
     products = jnp.zeros((2 * count, count), jnp.float32)
     for k in range(share):
         for lev in range(levels):
-            s = total[k, lev]
-            both = jnp.concatenate([ext[base + REACH + k, lev], s], axis=0)
-            products = products + dot_t(both, s)
+            s = split(total[k, lev])
+            o = split(ext[base + REACH + k, lev])
+            left = jnp.concatenate([o[0], s[0], o[1], s[1], o[2], s[2]], axis=0)
+            right = jnp.concatenate(s, axis=0)
+            nine = lax.dot_general(
+                left, right, (((1,), (1,)), ((), ())), preferred_element_type=jnp.float32
+            )
+            part = nine[: 2 * count, 2 * count :]
+            part = part + nine[2 * count : 4 * count, count : 2 * count]
+            part = part + nine[4 * count :, :count]
+            part = part + nine[: 2 * count, count : 2 * count]
+            part = part + nine[2 * count : 4 * count, :count]
+            products = products + (part + nine[: 2 * count, :count])
 
     half = count // 2
 

time: 51.5 us -> 50.8 us (0.986)
  Pallas kernels: 46.5 us -> 45.8 us
    pallas_call x1, Pallas kernels: 46.5 us -> 45.8 us  [on_device(): pl.pallas_call(functools.partial(sketch_kernel, n, ns, rows, math.sqrt(le...]
where the time goes in v5:
time: 50.8 us; the launch traced here: 50.5 us
  Pallas kernels  45.8 us (90%)
  local copies, waits for them, and re-layouts  3.47 us (7%)
  between operations  1.29 us (3%)
    pallas_call x1, Pallas kernels, on_device(): pl.pallas_call(functools.partial(sketch_kernel, n, ns, rows, math.sqrt(le...  45.8 us
    unnamed x2, local copies, waits for them, and re-layouts  3.47 us

profile of v5, /device:TPU:0, one launch (start us, length us, event | category | flops | bytes accessed | tf_op | source)
XLA Modules:
  0.0 50.5 jit_solution(17565678341601039222)
XLA Ops:
  1.3 45.8 %shard_map.68 = (f32[16,4,8,256]{3,2,1,0:T(8,128)}, f32[32,32]{1,0:T(8,128)}) custom-call(f32[32,4,16,256]{3,2,1,0:T(8,128)} %probes_ref.1, f32[16,16,256]{2,1,0:T(8,128)} %bitcast.3, s32[1,256]{1,0:T(1,128)} %cells_ref.1, s32[1,1]{1,0:T(1,128)S(6)} %copy.9.live_ref, f32[1,256]{1,0:T(1,128)} %weight_ref.1), custom_call_target="tpu_custom_call" | custom-call | tf_op jit(solution)/shard_map/pallas_call | solution.py:451
  47.1 2.1 %copy.7 = f32[8,4,16,256]{3,2,1,0:T(8,128)} copy(f32[8,4,16,256]{3,0,1,2:T(8,128)} %bitcast.2) | data formatting | bytes 1048576
  49.2 1.3 %copy.10 = f32[32,32]{1,0:T(8,128)} copy(f32[32,32]{1,0:T(8,128)} %get-tuple-element.11) | data formatting | bytes 8192
